TPU v7x, 32 devices: a whole 2x2x4 slice. The times are simulated.
32 devices in a mesh: slab: 16 (over z, x, core), shell: 2 (over y).
Axes of the slice: x: 2, y: 2, z: 4, core: 2. Of those that a mesh axis runs over, the one named last changes fastest.
Arguments:
- images: bfloat16 [2048, 2, 16384], P('slab', None, 'shell'), may hold values from -6 to 6
- defocus: bfloat16 [2048], P('slab'), may hold values from 20 to 200
- pose_bin: int32 [2048, 1], P('slab'), may hold values from 0 to 15; in each aligned block of 128 rows (0 to 127, 128 to 255, ...) at most 24 rows name the same one
- freq_sq: float32 [16384], P('shell'), may hold values from 0 to 1, as said below
- model_slice: float32 [16, 2, 16384], P('slab', None, 'shell'), may hold values from -6 to 6
- interp_coef: bfloat16 [16, 128, 4, 128, 128], P('slab', 'shell'), may hold values from -0.5 to 0.5
- block_index: int32 [16, 128, 4], P('slab', 'shell'), may hold values from 0 to 127, as said below
Outputs:
- volume_grad: float32 [128, 2, 128], P(('slab', 'shell'))
Inputs may be any that keep to these rules, and one draw needn't show every extreme that they name: `pose_bin`: among the images of one index of slab, no pose bin is named by more than 24 images, a bound that some block reaches. `freq_sq`: band s of the 2 bands of samples holds values between (s / 2) squared and ((s + 1) / 2) squared. `block_index`: among the 256 dense blocks of one pose bin in one shell band, the volume blocks v with the same v // 8 are named at most 32 times, and one such group exactly 32 times.
All inputs are finite; a program needn't handle non-finite values.
Results may differ from a plain program's by a relative error of at most 0.0029.
Values may be sent and summed in bfloat16 or wider, within the bound.
No kernel may reach another device: no remote copies, remote signals or barrier semaphores. Data moves between devices by JAX's collectives and lax.ppermute only.
A program may use at most 64 MiB of HBM per device.

v0:
```python
import functools
import math

import jax
import jax.numpy as jnp
import numpy as np
from jax import lax
from jax.experimental import pallas as pl
from jax.experimental.pallas import tpu as pltpu
from jax.sharding import PartitionSpec as P

f32 = jnp.float32
bf16 = jnp.bfloat16
LANES = 128
GROUP = 8
ROUND = 12582912.0


def sine_coefficients():
    x = np.cos(np.pi * (np.arange(400) + 0.5) / 400)
    cheb = np.polynomial.chebyshev.Chebyshev.fit(x, np.sin(np.pi * x), 11, domain=[-1, 1])
    power = cheb.convert(kind=np.polynomial.Polynomial).coef
    return [float(power[2 * n + 1] * 2.0 ** (2 * n + 1)) for n in range(6)]


SINE = sine_coefficients()


def sine_of_turns(turns):
    r = turns - ((turns + ROUND) - ROUND)
    q = r * r
    s = q * SINE[5] + SINE[4]
    for n in (3, 2, 1, 0):
        s = s * q + SINE[n]
    return s * r


def sums_kernel(
    half,
    unroll,
    pose_hbm,
    images_hbm,
    defocus_hbm,
    freq_hbm,
    model_hbm,
    index_hbm,
    coef_hbm,
    acc,
    other_ref,
    model_out,
    index_out,
    coef_out,
    pose,
    images,
    defocus,
    turns,
    spread,
    small_sems,
    image_sems,
    late_sems,
):
    count = images.shape[0]
    blocks = turns.shape[0]
    small = [
        pltpu.make_async_copy(src, dst, small_sems.at[n])
        for n, (src, dst) in enumerate(((pose_hbm, pose), (defocus_hbm, defocus), (freq_hbm, turns)))
    ]
    for copy in small:
        copy.start()

    def image_copy(j):
        rows = pl.ds(j * unroll, unroll)
        return pltpu.make_async_copy(images_hbm.at[rows], images.at[rows], image_sems.at[j])

    for j in range(count // unroll):
        image_copy(j).start()
    late = [
        pltpu.make_async_copy(src, dst, late_sems.at[n])
        for n, (src, dst) in enumerate(
            ((model_hbm, model_out), (index_hbm, index_out), (coef_hbm, coef_out))
        )
    ]
    for copy in late:
        copy.start()

    acc[...] = jnp.zeros_like(acc)
    rows = lax.broadcasted_iota(jnp.int32, (2 * blocks, 2 * blocks), 0)
    cols = lax.broadcasted_iota(jnp.int32, (2 * blocks, 2 * blocks), 1)
    apart = jnp.where(cols == 2 * (rows % blocks) + rows // blocks, 1.0, 0.0).astype(bf16)
    rows = lax.broadcasted_iota(jnp.int32, (count, count), 0)
    cols = lax.broadcasted_iota(jnp.int32, (count, count), 1)
    for copy in small:
        copy.wait()
    diagonal = jnp.where(rows == cols, defocus[...].astype(f32), 0.0).astype(bf16)
    spread[...] = jnp.dot(diagonal, jnp.ones((count, LANES), bf16), preferred_element_type=f32)
    turns[...] = turns[...] * (0.5 / math.pi)
    side = lax.axis_index("slab") & 1

    def one(image):
        s = sine_of_turns(spread[pl.ds(image, 1), :] * turns[...])
        both = jnp.dot(apart, images[image], preferred_element_type=f32)
        bin_ = pose[image]
        slot = ((bin_ & 1) ^ side) * half + (bin_ >> 1)
        return slot, s, both

    def body(j, _):
        image_copy(j).wait()
        for slot, s, both in [one(unroll * j + k) for k in range(unroll)]:
            old = acc[slot]
            acc[slot] = old + jnp.concatenate([s * both[:blocks], s * both[blocks:], s * s], axis=0)
        return 0

    lax.fori_loop(0, count // unroll, body, 0)
    other_ref[...] = acc[half:].astype(other_ref.dtype)
    for copy in late:
        copy.wait()


def weighted_sums(images, defocus, pose_bin, freq_sq, model_slice, interp_coef, block_index, bins):
    count, _, width = images.shape
    blocks = width // LANES
    half = bins // 2
    unroll = 16
    rows = images.reshape(count, 2, blocks, LANES).transpose(0, 2, 1, 3).reshape(count, 2 * blocks, LANES)
    model = model_slice.reshape(2, blocks, LANES).transpose(1, 0, 2).reshape(2 * blocks, LANES)
    index = block_index[0].T
    coef = interp_coef[0]
    hbm = pl.BlockSpec(memory_space=pltpu.HBM)
    vmem = pl.BlockSpec(memory_space=pltpu.VMEM)
    shapes = [
        ((bins, 3 * blocks, LANES), f32),
        ((half, 3 * blocks, LANES), bf16),
        (model.shape, f32),
        (index.shape, jnp.int32),
        (coef.shape, bf16),
    ]
    return pl.pallas_call(
        functools.partial(sums_kernel, half, unroll),
        in_specs=[hbm] * 7,
        out_specs=[vmem] * 5,
        out_shape=[jax.ShapeDtypeStruct(shape, dtype) for shape, dtype in shapes],
        scratch_shapes=[
            pltpu.SMEM((count,), jnp.int32),
            pltpu.VMEM(rows.shape, bf16),
            pltpu.VMEM((1, count), bf16),
            pltpu.VMEM((blocks, LANES), f32),
            pltpu.VMEM((count, LANES), f32),
            pltpu.SemaphoreType.DMA((3,)),
            pltpu.SemaphoreType.DMA((count // unroll,)),
            pltpu.SemaphoreType.DMA((3,)),
        ],
        compiler_params=pltpu.CompilerParams(vmem_limit_bytes=24 * 2**20),
    )(*[pltpu.with_memory_space_constraint(a, pltpu.HBM) for a in (pose_bin.reshape(-1), rows, defocus.reshape(1, -1), freq_sq.reshape(blocks, LANES), model, index, coef)])


def volume_kernel(scale, sums_ref, model_ref, index_ref, coef_ref, out_ref, residual, terms):
    blocks, touched = coef_ref.shape[:2]
    total = sums_ref[0].astype(f32)
    for part in range(1, sums_ref.shape[0]):
        total = total + sums_ref[part].astype(f32)
    power = total[2 * blocks :]
    for c in range(2):
        model = model_ref[pl.ds(c, blocks, 2), :]
        residual[c] = (power * model - total[c * blocks : (c + 1) * blocks]) * scale

    row = lax.broadcasted_iota(jnp.int32, (GROUP, LANES), 0)
    for first in range(0, blocks, GROUP):
        left = jnp.concatenate(
            [
                jnp.concatenate(
                    [jnp.where(row == m, residual[c, first : first + GROUP], 0.0) for m in range(GROUP)],
                    axis=1,
                )
                for c in range(2)
            ],
            axis=0,
        ).astype(bf16)
        for j in range(touched):
            right = coef_ref[first : first + GROUP, j].reshape(GROUP * LANES, LANES)
            got = jnp.dot(left, right, preferred_element_type=f32)
            for c in range(2):
                terms[j, first : first + GROUP, c * LANES : (c + 1) * LANES] = got[c * GROUP : (c + 1) * GROUP]

    volume = out_ref.shape[0]
    rows = lax.broadcasted_iota(jnp.int32, (volume, blocks), 0)
    total = jnp.zeros(out_ref.shape, f32)
    for j in range(touched):
        onehot = jnp.where(rows == index_ref[pl.ds(j, 1), :], 1.0, 0.0).astype(bf16)
        whole = terms[j]
        for _ in range(3):
            piece = whole.astype(bf16)
            whole = whole - piece.astype(f32)
            total = total + jnp.dot(onehot, piece, preferred_element_type=f32)
    out_ref[...] = total


def volume_share(sums, model, index, coef, volume, scale):
    blocks, touched = coef.shape[:2]
    vmem = pl.BlockSpec(memory_space=pltpu.VMEM)
    return pl.pallas_call(
        functools.partial(volume_kernel, scale),
        in_specs=[vmem] * 4,
        out_specs=vmem,
        out_shape=jax.ShapeDtypeStruct((volume, 2 * LANES), f32),
        scratch_shapes=[
            pltpu.VMEM((2, blocks, LANES), f32),
            pltpu.VMEM((touched, blocks, 2 * LANES), f32),
        ],
        compiler_params=pltpu.CompilerParams(vmem_limit_bytes=24 * 2**20),
    )(sums, model, index, coef)


def shards(images, defocus, pose_bin, freq_sq, model_slice, interp_coef, block_index, volume):
    slabs = lax.axis_size("slab")
    shells = lax.axis_size("shell")
    kept, other, model, index, coef = weighted_sums(
        images, defocus, pose_bin, freq_sq, model_slice, interp_coef, block_index, slabs
    )
    other = lax.ppermute(other, "slab", [(i, i ^ 1) for i in range(slabs)])
    pair = (kept[: slabs // 2] + other.astype(f32)).astype(bf16)
    sums = lax.all_to_all(
        pair,
        "slab",
        split_axis=0,
        concat_axis=0,
        tiled=True,
        axis_index_groups=[list(range(side, slabs, 2)) for side in range(2)],
    )
    share = volume_share(sums, model, index, coef, volume, 1.0 / images.shape[0])
    owned = volume // (slabs * shells)
    shares = lax.all_to_all(share, ("slab", "shell"), split_axis=0, concat_axis=0, tiled=True)
    return jnp.sum(shares.reshape(slabs * shells, owned, 2, LANES), axis=0)


def solution(mesh):
    owned = 4
    volume = owned * mesh.shape["slab"] * mesh.shape["shell"]
    return jax.shard_map(
        functools.partial(shards, volume=volume),
        mesh=mesh,
        in_specs=(
            P("slab", None, "shell"),
            P("slab"),
            P("slab", None),
            P("shell"),
            P("slab", None, "shell"),
            P("slab", "shell", None, None, None),
            P("slab", "shell", None),
        ),
        out_specs=P(("slab", "shell"), None, None),
        check_vma=False,
    )
```

profile of v0, /device:TPU:0, one launch (start us, length us, event | category | flops | bytes accessed | tf_op | source)
XLA Modules:
  0.0 41.4 jit_solution(3183484908454691040)
XLA Ops:
  0.0 6.1 %shard_map.73 = (f32[16,192,128]{2,1,0:T(8,128)S(1)}, bf16[8,192,128]{2,1,0:T(8,128)(2,1)S(1)}, f32[128,128]{1,0:T(8,128)S(1)}, s32[4,64]{1,0:T(4,128)S(1)}, bf16[64,4,128,128]{3,2,1,0:T(8,128)(2,1)S(1)}) custom-call(s32[128]{0:T(128)} %bitcast.22, bf16[128,128,128]{2,1,0:T(8,128)(2,1)} %bitcast.18, bf16[1,128]{1,0:T(2,128)(2,1)} %bitcast.23, ...), custom_call_target="tpu_custom_call" | custom-call | tf_op jit(solution)/shard_map/pallas_call | solution.py:137
  6.1 0.5 %collective-permute-start = (bf16[8,192,128]{2,1,0:T(8,128)(2,1)S(1)}, bf16[8,192,128]{2,1,0:T(8,128)(2,1)S(1)}, u32[]{:S(2)}, u32[]{:S(2)}) collective-permute-start(bf16[8,192,128]{2,1,0:T(8,128)(2,1)S(1)} %get-tuple-element.11), channel_id=1, source_target_pairs={{0,2},{2,0},{4,6},{6,4},{8,10},{10,8},{12,14},{14,12},{16,18},{18,... | collective-permute-start | bytes 1179656 | tf_op jit(solution)/shard_map/ppermute | solution.py:219
  6.7 1.3 %collective-permute-done = bf16[8,192,128]{2,1,0:T(8,128)(2,1)S(1)} collective-permute-done((bf16[8,192,128]{2,1,0:T(8,128)(2,1)S(1)}, bf16[8,192,128]{2,1,0:T(8,128)(2,1)S(1)}, u32[]{:S(2)}, u32[]{:S(2)}) %collective-permute-start) | collective-permute-done | bytes 393248 | tf_op jit(solution)/shard_map/ppermute | solution.py:219
  8.0 0.1 add_convert_fusion
  8.1 19.4 %all_to_all.14.sums_ref = bf16[8,192,128]{2,1,0:T(8,128)(2,1)S(1)} all-to-all(bf16[8,192,128]{2,1,0:T(8,128)(2,1)S(1)} %add_convert_fusion), channel_id=1, replica_groups={{0,4,8,12,16,20,24,28},{2,6,10,14,18,22,26,30},{1,5,9,13,17,21,25,29},{..., dimensions={0} | all-to-all | bytes 786432 | tf_op jit(solution)/shard_map/all_to_all | solution.py:221
  27.5 1.5 %shard_map.74 = f32[128,256]{1,0:T(8,128)S(1)} custom-call(bf16[8,192,128]{2,1,0:T(8,128)(2,1)S(1)} %all_to_all.14.sums_ref, f32[128,128]{1,0:T(8,128)S(1)} %get-tuple-element.12.model_ref, s32[4,64]{1,0:T(4,128)S(1)} %get-tuple-element.13.index_ref, bf16[64,4,128,128]{3,2,1,0:T(8,128)(2,1)S(1)} %get-tuple-element.14.coef_ref), custom_call_target="tpu_custom_call" | custom-call | tf_op jit(solution)/shard_map/pallas_call | solution.py:200
  29.0 11.7 %all_to_all.15 = f32[32,4,256]{2,1,0:T(4,128)S(1)} all-to-all(f32[32,4,256]{2,1,0:T(4,128)S(1)} %all_to_all.10), channel_id=1, replica_groups=mesh['slab'=16,'shell'=2] {'slab','shell'}, dimensions={0} | all-to-all | bytes 262144 | tf_op jit(solution)/shard_map/all_to_all | solution.py:231
  40.8 0.6 %reduce_sum.12 = f32[4,2,128]{2,1,0:T(2,128)} reshape(f32[4,256]{1,0:T(4,128)S(1)} %reduce_sum.11) | data formatting | bytes 8192 | tf_op jit(solution)/shard_map/reduce_sum | solution.py:232
  (2 shorter events, 0.1 us)
Async XLA Ops:
  6.1 1.9 %collective-permute-start = (bf16[8,192,128]{2,1,0:T(8,128)(2,1)S(1)}, bf16[8,192,128]{2,1,0:T(8,128)(2,1)S(1)}, u32[]{:S(2)}, u32[]{:S(2)}) collective-permute-start(bf16[8,192,128]{2,1,0:T(8,128)(2,1)S(1)} %get-tuple-element.11), channel_id=1, source_target_pairs={{0,2},{2,0},{4,6},{6,4},{8,10},{10,8},{12,14},{14,12},{16,18},{18,... | collective-permute-start | bytes 1179656 | tf_op jit(solution)/shard_map/ppermute | solution.py:219
where the time goes:
time: 41.6 us; the launch traced here: 41.4 us
  blocking collectives  31.1 us (75%)
  Pallas kernels  7.64 us (18%)
  waiting for transfers between devices  1.35 us (3%)
  local copies, waits for them, and re-layouts  0.65 us (2%)
  starting transfers between devices  0.52 us (1%)
    all_to_all x1, blocking collectives, shards(): lax.all_to_all(pair, 'slab', split_axis=0, concat_axis=0, tiled=True, axi...  19.4 us
    all_to_all x1, blocking collectives, shards(): lax.all_to_all(share, ('slab', 'shell'), split_axis=0, concat_axis=0, til...  11.7 us
    pallas_call x1, Pallas kernels, weighted_sums(): pl.pallas_call(functools.partial(sums_kernel, half, unroll), in_specs=[hb...  6.12 us
    pallas_call x1, Pallas kernels, volume_share(): pl.pallas_call(functools.partial(volume_kernel, scale), in_specs=[vmem] *...  1.52 us
    ppermute x1, waiting for transfers between devices, shards(): other = lax.ppermute(other, 'slab', [(i, i ^ 1) for i in range(slabs)])  1.35 us
  transfers between devices with their start and end apart: 1, of which 1 were waited for; matrix products, arithmetic and copies ran while one was open for 0% of the time, Pallas kernels for 0%

commit v1 on v0

--- a/solution.py
+++ b/solution.py
@@ -13,6 +13,11 @@
 bf16 = jnp.bfloat16
 LANES = 128
 GROUP = 8
+WAYS = 1
+LEAD = 2
+AHEAD = 1
+FINE = 64
+COARSE = 32
 ROUND = 12582912.0
 
 
@@ -35,83 +40,123 @@
     return s * r
 
 
+def fill_table(sines, cosines, turns):
+    count = sines.shape[0]
+    sines[0] = jnp.zeros_like(turns)
+    cosines[0] = jnp.ones_like(turns)
+    sines[1] = sine_of_turns(turns)
+    cosines[1] = sine_of_turns(turns + 0.25)
+    done = 2
+    while done < count:
+        last = done - 1
+        s, c = sines[last], cosines[last]
+        for n in range(1, min(done, count - last)):
+            sines[last + n] = s * cosines[n] + c * sines[n]
+            cosines[last + n] = c * cosines[n] - s * sines[n]
+        done += min(done, count - last) - 1
+
+
 def sums_kernel(
     half,
     unroll,
+    piece,
     pose_hbm,
     images_hbm,
     defocus_hbm,
     freq_hbm,
     model_hbm,
     index_hbm,
-    coef_hbm,
-    acc,
+    kept_ref,
     other_ref,
     model_out,
     index_out,
-    coef_out,
     pose,
     images,
     defocus,
-    turns,
-    spread,
+    freq,
+    steps,
+    step_row,
+    fine_sin,
+    fine_cos,
+    coarse_sin,
+    coarse_cos,
+    step_sem,
     small_sems,
     image_sems,
     late_sems,
+    *acc,
 ):
     count = images.shape[0]
-    blocks = turns.shape[0]
+    blocks = freq.shape[0]
     small = [
         pltpu.make_async_copy(src, dst, small_sems.at[n])
-        for n, (src, dst) in enumerate(((pose_hbm, pose), (defocus_hbm, defocus), (freq_hbm, turns)))
+        for n, (src, dst) in enumerate(((pose_hbm, pose), (defocus_hbm, defocus), (freq_hbm, freq)))
     ]
     for copy in small:
         copy.start()
 
     def image_copy(j):
-        rows = pl.ds(j * unroll, unroll)
+        rows = pl.ds(j * piece, piece)
         return pltpu.make_async_copy(images_hbm.at[rows], images.at[rows], image_sems.at[j])
 
-    for j in range(count // unroll):
+    lead = min(LEAD, count // piece)
+    for j in range(lead):
         image_copy(j).start()
     late = [
         pltpu.make_async_copy(src, dst, late_sems.at[n])
         for n, (src, dst) in enumerate(
-            ((model_hbm, model_out), (index_hbm, index_out), (coef_hbm, coef_out))
+            ((model_hbm, model_out), (index_hbm, index_out))
         )
     ]
-    for copy in late:
-        copy.start()
-
-    acc[...] = jnp.zeros_like(acc)
+
+    for part in acc:
+        part[...] = jnp.zeros_like(part)
     rows = lax.broadcasted_iota(jnp.int32, (2 * blocks, 2 * blocks), 0)
     cols = lax.broadcasted_iota(jnp.int32, (2 * blocks, 2 * blocks), 1)
     apart = jnp.where(cols == 2 * (rows % blocks) + rows // blocks, 1.0, 0.0).astype(bf16)
-    rows = lax.broadcasted_iota(jnp.int32, (count, count), 0)
-    cols = lax.broadcasted_iota(jnp.int32, (count, count), 1)
     for copy in small:
         copy.wait()
-    diagonal = jnp.where(rows == cols, defocus[...].astype(f32), 0.0).astype(bf16)
-    spread[...] = jnp.dot(diagonal, jnp.ones((count, LANES), bf16), preferred_element_type=f32)
-    turns[...] = turns[...] * (0.5 / math.pi)
+    for j in range(lead, count // piece):
+        image_copy(j).start()
+    for copy in late:
+        copy.start()
+    step_row[...] = (defocus[...].astype(f32) * 8.0).astype(jnp.int32)
+    step_copy = pltpu.make_async_copy(step_row.at[0], steps, step_sem)
+    step_copy.start()
+    fill_table(fine_sin, fine_cos, freq[...] * (0.0625 / math.pi))
+    fill_table(coarse_sin, coarse_cos, freq[...] * (4.0 / math.pi))
+    step_copy.wait()
     side = lax.axis_index("slab") & 1
 
     def one(image):
-        s = sine_of_turns(spread[pl.ds(image, 1), :] * turns[...])
+        u, v = steps[image] >> 6, steps[image] & (FINE - 1)
+        s = coarse_sin[u] * fine_cos[v] + coarse_cos[u] * fine_sin[v]
         both = jnp.dot(apart, images[image], preferred_element_type=f32)
         bin_ = pose[image]
         slot = ((bin_ & 1) ^ side) * half + (bin_ >> 1)
         return slot, s, both
 
     def body(j, _):
-        image_copy(j).wait()
-        for slot, s, both in [one(unroll * j + k) for k in range(unroll)]:
-            old = acc[slot]
-            acc[slot] = old + jnp.concatenate([s * both[:blocks], s * both[blocks:], s * s], axis=0)
+        for k in range(unroll // piece):
+            image_copy(j * (unroll // piece) + k).wait()
+        ready = []
+        for k in range(unroll + AHEAD):
+            if k < unroll:
+                ready.append(one(unroll * j + k))
+            if k >= AHEAD:
+                slot, s, both = ready.pop(0)
+                for part, value in enumerate((s * both[:blocks], s * both[blocks:], s * s)):
+                    acc[3 * (k % WAYS) + part][slot] += value
         return 0
 
     lax.fori_loop(0, count // unroll, body, 0)
-    other_ref[...] = acc[half:].astype(other_ref.dtype)
+    for part in range(3):
+        rows = slice(part * blocks, (part + 1) * blocks)
+        whole = acc[part][...]
+        for way in range(1, WAYS):
+            whole = whole + acc[3 * way + part][...]
+        kept_ref[:, rows] = whole[:half]
+        other_ref[:, rows] = whole[half:].astype(other_ref.dtype)
     for copy in late:
         copy.wait()
 
@@ -120,37 +165,43 @@
     count, _, width = images.shape
     blocks = width // LANES
     half = bins // 2
-    unroll = 16
+    unroll, piece = 16, 16
     rows = images.reshape(count, 2, blocks, LANES).transpose(0, 2, 1, 3).reshape(count, 2 * blocks, LANES)
     model = model_slice.reshape(2, blocks, LANES).transpose(1, 0, 2).reshape(2 * blocks, LANES)
     index = block_index[0].T
-    coef = interp_coef[0]
     hbm = pl.BlockSpec(memory_space=pltpu.HBM)
     vmem = pl.BlockSpec(memory_space=pltpu.VMEM)
     shapes = [
-        ((bins, 3 * blocks, LANES), f32),
+        ((half, 3 * blocks, LANES), f32),
         ((half, 3 * blocks, LANES), bf16),
         (model.shape, f32),
         (index.shape, jnp.int32),
-        (coef.shape, bf16),
     ]
     return pl.pallas_call(
-        functools.partial(sums_kernel, half, unroll),
-        in_specs=[hbm] * 7,
-        out_specs=[vmem] * 5,
+        functools.partial(sums_kernel, half, unroll, piece),
+        in_specs=[hbm] * 6,
+        out_specs=[vmem] * 4,
         out_shape=[jax.ShapeDtypeStruct(shape, dtype) for shape, dtype in shapes],
         scratch_shapes=[
             pltpu.SMEM((count,), jnp.int32),
             pltpu.VMEM(rows.shape, bf16),
             pltpu.VMEM((1, count), bf16),
             pltpu.VMEM((blocks, LANES), f32),
-            pltpu.VMEM((count, LANES), f32),
+            pltpu.SMEM((count,), jnp.int32),
+            pltpu.VMEM((1, count), jnp.int32),
+            pltpu.VMEM((FINE, blocks, LANES), f32),
+            pltpu.VMEM((FINE, blocks, LANES), f32),
+            pltpu.VMEM((COARSE, blocks, LANES), f32),
+            pltpu.VMEM((COARSE, blocks, LANES), f32),
+            pltpu.SemaphoreType.DMA,
             pltpu.SemaphoreType.DMA((3,)),
-            pltpu.SemaphoreType.DMA((count // unroll,)),
+            pltpu.SemaphoreType.DMA((count // piece,)),
             pltpu.SemaphoreType.DMA((3,)),
-        ],
+        ]
+        + [pltpu.VMEM((bins, blocks, LANES), f32)] * (3 * WAYS),
+        cost_estimate=pl.CostEstimate(flops=20*10**9, bytes_accessed=16*10**6, transcendentals=0),
         compiler_params=pltpu.CompilerParams(vmem_limit_bytes=24 * 2**20),
-    )(*[pltpu.with_memory_space_constraint(a, pltpu.HBM) for a in (pose_bin.reshape(-1), rows, defocus.reshape(1, -1), freq_sq.reshape(blocks, LANES), model, index, coef)])
+    )(*[pltpu.with_memory_space_constraint(a, pltpu.HBM) for a in (pose_bin.reshape(-1), rows, defocus.reshape(1, -1), freq_sq.reshape(blocks, LANES), model, index)])
 
 
 def volume_kernel(scale, sums_ref, model_ref, index_ref, coef_ref, out_ref, residual, terms):
@@ -213,11 +264,11 @@
 def shards(images, defocus, pose_bin, freq_sq, model_slice, interp_coef, block_index, volume):
     slabs = lax.axis_size("slab")
     shells = lax.axis_size("shell")
-    kept, other, model, index, coef = weighted_sums(
+    kept, other, model, index = weighted_sums(
         images, defocus, pose_bin, freq_sq, model_slice, interp_coef, block_index, slabs
     )
     other = lax.ppermute(other, "slab", [(i, i ^ 1) for i in range(slabs)])
-    pair = (kept[: slabs // 2] + other.astype(f32)).astype(bf16)
+    pair = (kept + other.astype(f32)).astype(bf16)
     sums = lax.all_to_all(
         pair,
         "slab",
@@ -226,7 +277,7 @@
         tiled=True,
         axis_index_groups=[list(range(side, slabs, 2)) for side in range(2)],
     )
-    share = volume_share(sums, model, index, coef, volume, 1.0 / images.shape[0])
+    share = volume_share(sums, model, index, interp_coef[0], volume, 1.0 / images.shape[0])
     owned = volume // (slabs * shells)
     shares = lax.all_to_all(share, ("slab", "shell"), split_axis=0, concat_axis=0, tiled=True)
     return jnp.sum(shares.reshape(slabs * shells, owned, 2, LANES), axis=0)

time: 41.6 us -> 40.3 us (0.969)
  Pallas kernels: 7.64 us -> 6.33 us
    pallas_call x1, Pallas kernels: 6.12 us -> 4.81 us  [weighted_sums(): pl.pallas_call(functools.partial(sums_kernel, half, unroll, piece), in_sp...]
where the time goes in v1:
time: 40.3 us; the launch traced here: 40.1 us
  blocking collectives  31.1 us (77%)
  Pallas kernels  6.33 us (16%)
  waiting for transfers between devices  1.35 us (3%)
  local copies, waits for them, and re-layouts  0.65 us (2%)
  starting transfers between devices  0.49 us (1%)
    all_to_all x1, blocking collectives, shards(): lax.all_to_all(pair, 'slab', split_axis=0, concat_axis=0, tiled=True, axi...  19.3 us
    all_to_all x1, blocking collectives, shards(): lax.all_to_all(share, ('slab', 'shell'), split_axis=0, concat_axis=0, til...  11.7 us
    pallas_call x1, Pallas kernels, weighted_sums(): pl.pallas_call(functools.partial(sums_kernel, half, unroll, piece), in_sp...  4.81 us
    pallas_call x1, Pallas kernels, volume_share(): pl.pallas_call(functools.partial(volume_kernel, scale), in_specs=[vmem] *...  1.52 us
    ppermute x1, waiting for transfers between devices, shards(): other = lax.ppermute(other, 'slab', [(i, i ^ 1) for i in range(slabs)])  1.35 us
  transfers between devices with their start and end apart: 1, of which 1 were waited for; matrix products, arithmetic and copies ran while one was open for 0% of the time, Pallas kernels for 0%

profile of v1, /device:TPU:0, one launch (start us, length us, event | category | flops | bytes accessed | tf_op | source)
XLA Modules:
  0.0 40.1 jit_solution(12067317146090921976)
XLA Ops:
  0.0 0.0 copy-start
  0.0 4.8 %shard_map.73 = (f32[8,192,128]{2,1,0:T(8,128)S(1)}, bf16[8,192,128]{2,1,0:T(8,128)(2,1)S(1)}, f32[128,128]{1,0:T(8,128)S(1)}, s32[4,64]{1,0:T(4,128)S(1)}) custom-call(s32[128]{0:T(128)} %bitcast.22, bf16[128,128,128]{2,1,0:T(8,128)(2,1)} %bitcast.18, bf16[1,128]{1,0:T(2,128)(2,1)} %bitcast.23, f32[64,128]{1,0:T(8,128)} %bitcast.20, f32[128,128]{1,0:T(8,128)} %bitcast.19, ...), custom_call_target="tpu_custom_call" | custom-call | flops 20000000000 | bytes 16000000 | tf_op jit(solution)/shard_map/pallas_call | solution.py:180
  4.8 0.5 %collective-permute-start = (bf16[8,192,128]{2,1,0:T(8,128)(2,1)S(1)}, bf16[8,192,128]{2,1,0:T(8,128)(2,1)S(1)}, u32[]{:S(2)}, u32[]{:S(2)}) collective-permute-start(bf16[8,192,128]{2,1,0:T(8,128)(2,1)S(1)} %get-tuple-element.10), channel_id=1, source_target_pairs={{0,2},{2,0},{4,6},{6,4},{8,10},{10,8},{12,14},{14,12},{16,18},{18,... | collective-permute-start | bytes 1179656 | tf_op jit(solution)/shard_map/ppermute | solution.py:270
  5.3 1.3 %collective-permute-done = bf16[8,192,128]{2,1,0:T(8,128)(2,1)S(1)} collective-permute-done((bf16[8,192,128]{2,1,0:T(8,128)(2,1)S(1)}, bf16[8,192,128]{2,1,0:T(8,128)(2,1)S(1)}, u32[]{:S(2)}, u32[]{:S(2)}) %collective-permute-start) | collective-permute-done | bytes 393248 | tf_op jit(solution)/shard_map/ppermute | solution.py:270
  6.7 0.1 add_convert_fusion
  6.8 19.3 %all_to_all.14.sums_ref = bf16[8,192,128]{2,1,0:T(8,128)(2,1)S(1)} all-to-all(bf16[8,192,128]{2,1,0:T(8,128)(2,1)S(1)} %add_convert_fusion), channel_id=1, replica_groups={{0,4,8,12,16,20,24,28},{2,6,10,14,18,22,26,30},{1,5,9,13,17,21,25,29},{..., dimensions={0} | all-to-all | bytes 786432 | tf_op jit(solution)/shard_map/all_to_all | solution.py:272
  26.1 0.0 copy-done
  26.1 1.5 %shard_map.74 = f32[128,256]{1,0:T(8,128)S(1)} custom-call(bf16[8,192,128]{2,1,0:T(8,128)(2,1)S(1)} %all_to_all.14.sums_ref, f32[128,128]{1,0:T(8,128)S(1)} %get-tuple-element.11.model_ref, s32[4,64]{1,0:T(4,128)S(1)} %get-tuple-element.12.index_ref, bf16[64,4,128,128]{3,2,1,0:T(8,128)(2,1)S(1)} %bitcast.17), custom_call_target="tpu_custom_call" | custom-call | tf_op jit(solution)/shard_map/pallas_call | solution.py:251
  27.7 11.7 %all_to_all.15 = f32[32,4,256]{2,1,0:T(4,128)S(1)} all-to-all(f32[32,4,256]{2,1,0:T(4,128)S(1)} %all_to_all.10), channel_id=1, replica_groups=mesh['slab'=16,'shell'=2] {'slab','shell'}, dimensions={0} | all-to-all | bytes 262144 | tf_op jit(solution)/shard_map/all_to_all | solution.py:282
  39.5 0.6 %reduce_sum.12 = f32[4,2,128]{2,1,0:T(2,128)} reshape(f32[4,256]{1,0:T(4,128)S(1)} %reduce_sum.11) | data formatting | bytes 8192 | tf_op jit(solution)/shard_map/reduce_sum | solution.py:283
  (2 shorter events, 0.1 us)
Async XLA Ops:
  0.0 26.1 %copy-start = (bf16[1,64,4,128,128]{4,3,2,1,0:T(8,128)(2,1)S(1)}, bf16[1,64,4,128,128]{4,3,2,1,0:T(8,128)(2,1)}, u32[]{:S(2)}) copy-start(bf16[1,64,4,128,128]{4,3,2,1,0:T(8,128)(2,1)} %param.12) | copy-start | bytes 25165828
  4.8 1.8 %collective-permute-start = (bf16[8,192,128]{2,1,0:T(8,128)(2,1)S(1)}, bf16[8,192,128]{2,1,0:T(8,128)(2,1)S(1)}, u32[]{:S(2)}, u32[]{:S(2)}) collective-permute-start(bf16[8,192,128]{2,1,0:T(8,128)(2,1)S(1)} %get-tuple-element.10), channel_id=1, source_target_pairs={{0,2},{2,0},{4,6},{6,4},{8,10},{10,8},{12,14},{14,12},{16,18},{18,... | collective-permute-start | bytes 1179656 | tf_op jit(solution)/shard_map/ppermute | solution.py:270

commit v2 on v1

v2 whole, which is shorter than its diff:
```python
import functools
import math

import jax
import jax.numpy as jnp
import numpy as np
from jax import lax
from jax.experimental import pallas as pl
from jax.experimental.pallas import tpu as pltpu
from jax.sharding import PartitionSpec as P

f32 = jnp.float32
bf16 = jnp.bfloat16
LANES = 128
GROUP = 8
LEAD = 2
FINE = 64
COARSE = 32
COUNT_ROWS = 16
ROUND = 12582912.0


HBM = pl.BlockSpec(memory_space=pltpu.HBM)
VMEM = pl.BlockSpec(memory_space=pltpu.VMEM)


def sine_coefficients():
    x = np.cos(np.pi * (np.arange(400) + 0.5) / 400)
    cheb = np.polynomial.chebyshev.Chebyshev.fit(x, np.sin(np.pi * x), 11, domain=[-1, 1])
    power = cheb.convert(kind=np.polynomial.Polynomial).coef
    return [float(power[2 * n + 1] * 2.0 ** (2 * n + 1)) for n in range(6)]


SINE = sine_coefficients()


def sine_of_turns(turns):
    r = turns - ((turns + ROUND) - ROUND)
    q = r * r
    s = q * SINE[5] + SINE[4]
    for n in (3, 2, 1, 0):
        s = s * q + SINE[n]
    return s * r


def in_hbm(arrays):
    return [pltpu.with_memory_space_constraint(a, pltpu.HBM) for a in arrays]


def fill_table(sines, cosines, turns):
    count = sines.shape[0]
    sines[0] = jnp.zeros_like(turns)
    cosines[0] = jnp.ones_like(turns)
    sines[1] = sine_of_turns(turns)
    cosines[1] = sine_of_turns(turns + 0.25)
    done = 2
    while done < count:
        last = done - 1
        s, c = sines[last], cosines[last]
        for n in range(1, min(done, count - last)):
            sines[last + n] = s * cosines[n] + c * sines[n]
            cosines[last + n] = c * cosines[n] - s * sines[n]
        done += min(done, count - last) - 1


def sums_kernel(
    half,
    unroll,
    piece,
    pose_hbm,
    images_hbm,
    defocus_hbm,
    freq_hbm,
    kept_ref,
    other_ref,
    fine_sin,
    fine_cos,
    coarse_sin,
    coarse_cos,
    freq,
    pose,
    pose_row,
    images,
    defocus,
    steps,
    step_row,
    step_sem,
    small_sems,
    image_sems,
    counts,
    *acc,
):
    count = images.shape[0]
    blocks = freq.shape[0]
    small = [
        pltpu.make_async_copy(src, dst, small_sems.at[n])
        for n, (src, dst) in enumerate(((defocus_hbm, defocus), (freq_hbm, freq), (pose_hbm.at[0], pose), (pose_hbm, pose_row)))
    ]
    for copy in small:
        copy.start()

    def image_copy(j):
        rows = pl.ds(j * piece, piece)
        return pltpu.make_async_copy(images_hbm.at[rows], images.at[rows], image_sems.at[j])

    lead = min(LEAD, count // piece)
    for j in range(lead):
        image_copy(j).start()
    for part in acc:
        part[...] = jnp.zeros_like(part)
    rows = lax.broadcasted_iota(jnp.int32, (2 * blocks, 2 * blocks), 0)
    cols = lax.broadcasted_iota(jnp.int32, (2 * blocks, 2 * blocks), 1)
    apart = jnp.where(cols == 2 * (rows % blocks) + rows // blocks, 1.0, 0.0).astype(bf16)
    for copy in small:
        copy.wait()
    for j in range(lead, count // piece):
        image_copy(j).start()
    side = lax.axis_index("slab") & 1
    step_row[...] = (defocus[...].astype(f32) * 8.0).astype(jnp.int32)
    step_copy = pltpu.make_async_copy(step_row.at[0], steps, step_sem)
    step_copy.start()
    fill_table(fine_sin, fine_cos, freq[...] * (0.0625 / math.pi))
    fill_table(coarse_sin, coarse_cos, freq[...] * (4.0 / math.pi))
    rows = lax.broadcasted_iota(jnp.int32, (count, count), 0)
    cols = lax.broadcasted_iota(jnp.int32, (count, count), 1)
    diagonal = jnp.where(rows == cols, defocus[...].astype(f32), 0.0).astype(bf16)
    spread = jnp.dot(diagonal, jnp.ones((count, LANES), bf16), preferred_element_type=f32)
    eighths = (spread * 8.0).astype(jnp.int32)
    bins = 2 * half
    place = ((pose_row[...] & 1) ^ side) * half + (pose_row[...] >> 1)
    place = place * COUNT_ROWS + (step_row[...] >> 7)
    chosen = lax.broadcasted_iota(jnp.int32, (bins * COUNT_ROWS, count), 0) == place
    chosen = jnp.where(chosen, 1.0, 0.0).astype(bf16)
    named = (eighths & (LANES - 1)) == lax.broadcasted_iota(jnp.int32, (count, LANES), 1)
    named = jnp.where(named, 1.0, 0.0).astype(bf16)
    counts[...] = jnp.dot(chosen, named, preferred_element_type=f32)
    step_copy.wait()

    def one(image):
        u, v = steps[image] >> 6, steps[image] & (FINE - 1)
        s = coarse_sin[u] * fine_cos[v] + coarse_cos[u] * fine_sin[v]
        both = jnp.dot(apart, images[image], preferred_element_type=f32)
        bin_ = pose[image]
        slot = ((bin_ & 1) ^ side) * half + (bin_ >> 1)
        return slot, s, both

    def body(j, _):
        for k in range(unroll // piece):
            image_copy(j * (unroll // piece) + k).wait()
        for k in range(unroll):
            slot, s, both = one(unroll * j + k)
            for part, value in enumerate((s * both[:blocks], s * both[blocks:])):
                acc[part][slot] += value
        return 0

    lax.fori_loop(0, count // unroll, body, 0)
    numbers = counts[...].reshape(bins, COUNT_ROWS, LANES)
    for first, part in ((0, acc[0][...]), (blocks, acc[1][...]), (2 * blocks, numbers)):
        rows = slice(first, first + part.shape[1])
        kept_ref[:, rows] = part[:half]
        other_ref[:, rows] = part[half:].astype(other_ref.dtype)


def weighted_sums(images, defocus, pose_bin, freq_sq, bins):
    count, _, width = images.shape
    blocks = width // LANES
    half = bins // 2
    unroll, piece = 32, 16
    rows = images.reshape(count, 2, blocks, LANES).transpose(0, 2, 1, 3).reshape(count, 2 * blocks, LANES)
    height = 2 * blocks + COUNT_ROWS
    return pl.pallas_call(
        functools.partial(sums_kernel, half, unroll, piece),
        in_specs=[HBM] * 4,
        out_specs=[VMEM] * 7,
        out_shape=[
            jax.ShapeDtypeStruct((half, height, LANES), f32),
            jax.ShapeDtypeStruct((half, height, LANES), bf16),
        ]
        + [jax.ShapeDtypeStruct((n, blocks, LANES), f32) for n in (FINE, FINE, COARSE, COARSE)]
        + [jax.ShapeDtypeStruct((blocks, LANES), f32)],
        scratch_shapes=[
            pltpu.SMEM((count,), jnp.int32),
            pltpu.VMEM((1, count), jnp.int32),
            pltpu.VMEM(rows.shape, bf16),
            pltpu.VMEM((1, count), bf16),
            pltpu.SMEM((count,), jnp.int32),
            pltpu.VMEM((1, count), jnp.int32),
            pltpu.SemaphoreType.DMA,
            pltpu.SemaphoreType.DMA((4,)),
            pltpu.SemaphoreType.DMA((count // piece,)),
            pltpu.VMEM((bins * COUNT_ROWS, LANES), f32),
            pltpu.VMEM((bins, blocks, LANES), f32),
            pltpu.VMEM((bins, blocks, LANES), f32),
        ],
        cost_estimate=pl.CostEstimate(flops=20 * 10**9, bytes_accessed=16 * 10**6, transcendentals=0),
        compiler_params=pltpu.CompilerParams(vmem_limit_bytes=24 * 2**20),
    )(*in_hbm([pose_bin.reshape(1, -1), rows, defocus.reshape(1, -1), freq_sq.reshape(blocks, LANES)]))


def turn_by(cosine, sine, by):
    return cosine * by[0] - sine * by[1], sine * by[0] + cosine * by[1]


def tables_kernel(
    model_hbm, index_hbm, fine_sin, fine_cos, coarse_sin, coarse_cos, freq, model, index, fine, coarse, sems
):
    blocks = index.shape[1]
    copies = [
        pltpu.make_async_copy(src, dst, sems.at[n])
        for n, (src, dst) in enumerate(((model_hbm, model), (index_hbm, index)))
    ]
    for copy in copies:
        copy.start()

    first = lax.broadcasted_iota(jnp.int32, (8, LANES), 0).astype(f32)

    def entry(cosines, sines, k, n):
        rows = pl.ds(n * blocks + k, 1)
        return cosines[rows, :], sines[rows, :]

    def one(k):
        lanes = [pl.ds(pl.multiple_of((2 * k + part) * LANES, LANES), LANES) for part in range(2)]
        f = freq[pl.ds(k, 1), :]
        angle = first * (f * (0.125 / math.pi))
        pair = [(sine_of_turns(angle + 0.25), sine_of_turns(angle))]
        by = entry(fine_cos, fine_sin, k, 16)
        for _ in range(FINE // 8 - 1):
            pair.append(turn_by(*pair[-1], by))
        for part in range(2):
            fine[:, lanes[part]] = jnp.concatenate([p[part] for p in pair], axis=0).astype(bf16)
        angle = first * (f * (16.0 / math.pi))
        angle = angle - ((angle + ROUND) - ROUND)
        even = (sine_of_turns(angle + 0.25), sine_of_turns(angle))
        by = entry(coarse_cos, coarse_sin, k, 16)
        pair = [even, turn_by(*even, turn_by(*by, by))]
        by = entry(coarse_cos, coarse_sin, k, 2)
        pair += [turn_by(*p, by) for p in pair]
        coarse[:, lanes[0]] = jnp.concatenate([p[0] for p in pair], axis=0)
        coarse[:, lanes[1]] = jnp.concatenate([-p[1] for p in pair], axis=0)

    def body(j, _):
        for k in range(GROUP):
            one(GROUP * j + k)
        return 0

    lax.fori_loop(0, blocks // GROUP, body, 0)
    for copy in copies:
        copy.wait()


def tables(angles, model_slice, block_index):
    blocks = block_index.shape[1]
    model = model_slice.reshape(2, blocks, LANES).transpose(1, 0, 2).reshape(2 * blocks, LANES)
    index = block_index[0].T
    shapes = [
        (model.shape, f32),
        (index.shape, jnp.int32),
        ((FINE, 2 * blocks * LANES), bf16),
        ((COARSE, 2 * blocks * LANES), f32),
    ]
    return pl.pallas_call(
        tables_kernel,
        in_specs=[HBM] * 2 + [VMEM] * 5,
        out_specs=[VMEM] * 4,
        out_shape=[jax.ShapeDtypeStruct(shape, dtype) for shape, dtype in shapes],
        scratch_shapes=[
            pltpu.SemaphoreType.DMA((2,)),
        ],
        cost_estimate=pl.CostEstimate(flops=10**9, bytes_accessed=10**6, transcendentals=0),
        compiler_params=pltpu.CompilerParams(vmem_limit_bytes=8 * 2**20),
    )(*in_hbm([model, index]), *[a.reshape(-1, LANES) for a in angles])


def volume_kernel(
    scale, sums_ref, model_ref, index_ref, fine, coarse, coef_ref, out_ref, power, residual, terms
):
    blocks, touched = coef_ref.shape[:2]
    total = sums_ref[0].astype(f32)
    for part in range(1, sums_ref.shape[0]):
        total = total + sums_ref[part].astype(f32)
    counts = total[2 * blocks :]
    counts = jnp.concatenate([counts, pltpu.roll(counts, FINE, 1)], axis=0)[:, :FINE]
    named = jnp.sum(counts)
    high = counts.astype(bf16)
    counts = jnp.concatenate([high, (counts - high.astype(f32)).astype(bf16)], axis=0)
    for first in range(0, blocks, GROUP):
        lanes = slice(2 * first * LANES, 2 * (first + GROUP) * LANES)
        inner = jnp.dot(counts, fine[:, lanes], preferred_element_type=f32)
        cosine = (inner[:COARSE] + inner[COARSE:]) * coarse[:, lanes]
        cosine = sum(cosine[n : n + 8] for n in range(0, COARSE, 8))
        for k in range(GROUP):
            both = cosine[:, 2 * k * LANES : (2 * k + 1) * LANES] + cosine[:, (2 * k + 1) * LANES : (2 * k + 2) * LANES]
            both = jnp.sum(both, axis=0, keepdims=True)
            power[first + k : first + k + 1, :] = (named - both) * 0.5

    for c in range(2):
        model = model_ref[pl.ds(c, blocks, 2), :]
        residual[c] = (power[...] * model - total[c * blocks : (c + 1) * blocks]) * scale

    row = lax.broadcasted_iota(jnp.int32, (GROUP, LANES), 0)
    for first in range(0, blocks, GROUP):
        left = jnp.concatenate(
            [
                jnp.concatenate(
                    [jnp.where(row == m, residual[c, first : first + GROUP], 0.0) for m in range(GROUP)],
                    axis=1,
                )
                for c in range(2)
            ],
            axis=0,
        ).astype(bf16)
        for j in range(touched):
            right = coef_ref[first : first + GROUP, j].reshape(GROUP * LANES, LANES)
            got = jnp.dot(left, right, preferred_element_type=f32)
            for c in range(2):
                terms[j, first : first + GROUP, c * LANES : (c + 1) * LANES] = got[c * GROUP : (c + 1) * GROUP]

    volume = out_ref.shape[0]
    rows = lax.broadcasted_iota(jnp.int32, (volume, blocks), 0)
    total = jnp.zeros(out_ref.shape, f32)
    for j in range(touched):
        onehot = jnp.where(rows == index_ref[pl.ds(j, 1), :], 1.0, 0.0).astype(bf16)
        whole = terms[j]
        for _ in range(3):
            piece = whole.astype(bf16)
            whole = whole - piece.astype(f32)
            total = total + jnp.dot(onehot, piece, preferred_element_type=f32)
    out_ref[...] = total


def volume_share(sums, loaded, coef, volume, scale):
    blocks, touched = coef.shape[:2]
    return pl.pallas_call(
        functools.partial(volume_kernel, scale),
        in_specs=[VMEM] * 6,
        out_specs=VMEM,
        out_shape=jax.ShapeDtypeStruct((volume, 2 * LANES), f32),
        scratch_shapes=[
            pltpu.VMEM((blocks, LANES), f32),
            pltpu.VMEM((2, blocks, LANES), f32),
            pltpu.VMEM((touched, blocks, 2 * LANES), f32),
        ],
        compiler_params=pltpu.CompilerParams(vmem_limit_bytes=16 * 2**20),
    )(sums, *loaded, coef)


def shards(images, defocus, pose_bin, freq_sq, model_slice, interp_coef, block_index, volume):
    slabs = lax.axis_size("slab")
    shells = lax.axis_size("shell")
    kept, other, *angles = weighted_sums(images, defocus, pose_bin, freq_sq, slabs)
    loaded = tables(angles, model_slice, block_index)
    other = lax.ppermute(other, "slab", [(i, i ^ 1) for i in range(slabs)])
    pair = (kept + other.astype(f32)).astype(bf16)
    pair, loaded = lax.optimization_barrier((pair, loaded))
    sums = lax.all_to_all(
        pair,
        "slab",
        split_axis=0,
        concat_axis=0,
        tiled=True,
        axis_index_groups=[list(range(side, slabs, 2)) for side in range(2)],
    )
    share = volume_share(sums, loaded, interp_coef[0], volume, 1.0 / images.shape[0])
    owned = volume // (slabs * shells)
    shares = lax.all_to_all(share, ("slab", "shell"), split_axis=0, concat_axis=0, tiled=True)
    return jnp.sum(shares.reshape(slabs * shells, owned, 2, LANES), axis=0)


def solution(mesh):
    owned = 4
    volume = owned * mesh.shape["slab"] * mesh.shape["shell"]
    return jax.shard_map(
        functools.partial(shards, volume=volume),
        mesh=mesh,
        in_specs=(
            P("slab", None, "shell"),
            P("slab"),
            P("slab", None),
            P("shell"),
            P("slab", None, "shell"),
            P("slab", "shell", None, None, None),
            P("slab", "shell", None),
        ),
        out_specs=P(("slab", "shell"), None, None),
        check_vma=False,
    )
```

time: 40.3 us -> 39.2 us (0.973)
  Pallas kernels: 6.33 us -> 8.65 us
  blocking collectives: 31.1 us -> 29 us
  waiting for transfers between devices: 1.35 us -> 0.01 us
    pallas_call x1 -> x2, Pallas kernels: 1.52 us -> 3.81 us  [the longest x1 2.2 us: volume_share(): pl.pallas_call(functools.partial(volume_kernel, scale), in_specs=[VMEM] *...]
    all_to_all x1, blocking collectives: 19.3 us -> 17.6 us  [shards(): lax.all_to_all(pair, 'slab', split_axis=0, concat_axis=0, tiled=True, axi...]
    ppermute x1, waiting for transfers between devices: 1.35 us -> 0.01 us  [shards(): other = lax.ppermute(other, 'slab', [(i, i ^ 1) for i in range(slabs)])]
    all_to_all x1, blocking collectives: 11.7 us -> 11.3 us  [shards(): lax.all_to_all(share, ('slab', 'shell'), split_axis=0, concat_axis=0, til...]
  transfers between devices with their start and end apart: 1 -> 1, of which waited for: 1 -> 0; matrix products, arithmetic and copies ran while one was open for 0% -> 0% of each run, Pallas kernels for 0% -> 4%
where the time goes in v2:
time: 39.2 us; the launch traced here: 38.9 us
  blocking collectives  29 us (74%)
  Pallas kernels  8.65 us (22%)
  local copies, waits for them, and re-layouts  0.65 us (2%)
  starting transfers between devices  0.51 us (1%)
    all_to_all x1, blocking collectives, shards(): lax.all_to_all(pair, 'slab', split_axis=0, concat_axis=0, tiled=True, axi...  17.6 us
    all_to_all x1, blocking collectives, shards(): lax.all_to_all(share, ('slab', 'shell'), split_axis=0, concat_axis=0, til...  11.3 us
    pallas_call x1, Pallas kernels, weighted_sums(): pl.pallas_call(functools.partial(sums_kernel, half, unroll, piece), in_sp...  4.84 us
    pallas_call x1, Pallas kernels, volume_share(): pl.pallas_call(functools.partial(volume_kernel, scale), in_specs=[VMEM] *...  2.2 us
    pallas_call x1, Pallas kernels, tables(): pl.pallas_call(tables_kernel, in_specs=[HBM] * 2 + [VMEM] * 5, out_specs=...  1.61 us
  transfers between devices with their start and end apart: 1, of which 0 were waited for; matrix products, arithmetic and copies ran while one was open for 0% of the time, Pallas kernels for 4%

profile of v2, /device:TPU:0, one launch (start us, length us, event | category | flops | bytes accessed | tf_op | source)
XLA Modules:
  0.0 38.9 jit_solution(4465848146745101776)
XLA Ops:
  0.0 0.0 copy-start
  0.0 4.8 %shard_map.73 = (f32[8,144,128]{2,1,0:T(8,128)S(1)}, bf16[8,144,128]{2,1,0:T(8,128)(2,1)S(1)}, f32[64,64,128]{2,1,0:T(8,128)S(1)}, f32[64,64,128]{2,1,0:T(8,128)...) custom-call(s32[1,128]{1,0:T(1,128)} %bitcast.30, ...), custom_call_target="tpu_custom_call" | custom-call | flops 20000000000 | bytes 16000000 | tf_op jit(solution)/shard_map/pallas_call | solution.py:171
  4.8 0.5 %collective-permute-start = (bf16[8,144,128]{2,1,0:T(8,128)(2,1)S(1)}, bf16[8,144,128]{2,1,0:T(8,128)(2,1)S(1)}, u32[]{:S(2)}, u32[]{:S(2)}) collective-permute-start(bf16[8,144,128]{2,1,0:T(8,128)(2,1)S(1)} %get-tuple-element.22), channel_id=1, source_target_pairs={{0,2},{2,0},{4,6},{6,4},{8,10},{10,8},{12,14},{14,12},{16,18},{18,... | collective-permute-start | bytes 884744 | tf_op jit(solution)/shard_map/ppermute | solution.py:352
  5.4 1.6 %shard_map.74 = (f32[128,128]{1,0:T(8,128)S(1)}, s32[4,64]{1,0:T(4,128)S(1)}, bf16[64,16384]{1,0:T(8,128)(2,1)S(1)}, f32[32,16384]{1,0:T(8,128)S(1)}) custom-call(f32[128,128]{1,0:T(8,128)} %bitcast.26, s32[4,64]{1,0:T(4,128)} %bitcast.27, f32[4096,128]{1,0:T(8,128)S(1)} %bitcast.22, f32[4096,128]{1,0:T(8,128)S(1)} %bitcast.23, f32[2048,128]{1,0:T(8,128)S(1)} %bitcast.24, ...), custom_call_target="tpu_custom_call" | custom-call | flops 1000000000 | bytes 1000000 | tf_op jit(solution)/shard_map/pallas_call | solution.py:261
  7.0 0.0 collective-permute-done
  7.0 0.1 add_convert_fusion
  7.1 17.6 %all_to_all.14.sums_ref = bf16[8,144,128]{2,1,0:T(8,128)(2,1)S(1)} all-to-all(bf16[8,144,128]{2,1,0:T(8,128)(2,1)S(1)} %add_convert_fusion), channel_id=1, replica_groups={{0,4,8,12,16,20,24,28},{2,6,10,14,18,22,26,30},{1,5,9,13,17,21,25,29},{..., dimensions={0} | all-to-all | bytes 589824 | tf_op jit(solution)/shard_map/all_to_all | solution.py:355
  24.7 0.0 copy-done
  24.7 2.2 %shard_map.75 = f32[128,256]{1,0:T(8,128)S(1)} custom-call(bf16[8,144,128]{2,1,0:T(8,128)(2,1)S(1)} %all_to_all.14.sums_ref, f32[128,128]{1,0:T(8,128)S(1)} %get-tuple-element.33.model_ref, s32[4,64]{1,0:T(4,128)S(1)} %get-tuple-element.34.index_ref, bf16[64,16384]{1,0:T(8,128)(2,1)S(1)} %get-tuple-element.35.fine, ...), custom_call_target="tpu_custom_call" | custom-call | tf_op jit(solution)/shard_map/pallas_call | solution.py:333
  27.0 11.3 %all_to_all.15 = f32[32,4,256]{2,1,0:T(4,128)S(1)} all-to-all(f32[32,4,256]{2,1,0:T(4,128)S(1)} %all_to_all.10), channel_id=1, replica_groups=mesh['slab'=16,'shell'=2] {'slab','shell'}, dimensions={0} | all-to-all | bytes 262144 | tf_op jit(solution)/shard_map/all_to_all | solution.py:365
  38.3 0.6 %reduce_sum.12 = f32[4,2,128]{2,1,0:T(2,128)} reshape(f32[4,256]{1,0:T(4,128)S(1)} %reduce_sum.11) | data formatting | bytes 8192 | tf_op jit(solution)/shard_map/reduce_sum | solution.py:366
  (2 shorter events, 0.1 us)
Async XLA Ops:
  0.0 24.7 %copy-start = (bf16[1,64,4,128,128]{4,3,2,1,0:T(8,128)(2,1)S(1)}, bf16[1,64,4,128,128]{4,3,2,1,0:T(8,128)(2,1)}, u32[]{:S(2)}) copy-start(bf16[1,64,4,128,128]{4,3,2,1,0:T(8,128)(2,1)} %param.12) | copy-start | bytes 25165828
  4.8 2.1 %collective-permute-start = (bf16[8,144,128]{2,1,0:T(8,128)(2,1)S(1)}, bf16[8,144,128]{2,1,0:T(8,128)(2,1)S(1)}, u32[]{:S(2)}, u32[]{:S(2)}) collective-permute-start(bf16[8,144,128]{2,1,0:T(8,128)(2,1)S(1)} %get-tuple-element.22), channel_id=1, source_target_pairs={{0,2},{2,0},{4,6},{6,4},{8,10},{10,8},{12,14},{14,12},{16,18},{18,... | collective-permute-start | bytes 884744 | tf_op jit(solution)/shard_map/ppermute | solution.py:352

commit v3 on v2

--- a/solution.py
+++ b/solution.py
@@ -16,6 +16,7 @@
 LEAD = 2
 FINE = 64
 COARSE = 32
+COARSE_USED = 26
 COUNT_ROWS = 16
 ROUND = 12582912.0
 
@@ -32,6 +33,28 @@
 
 
 SINE = sine_coefficients()
+
+
+def cosine_coefficients():
+    x = np.cos(np.pi * (np.arange(400) + 0.5) / 400)
+    cheb = np.polynomial.chebyshev.Chebyshev.fit(x, np.cos(np.pi * x), 12, domain=[-1, 1])
+    power = cheb.convert(kind=np.polynomial.Polynomial).coef
+    return [float(power[2 * n] * 4.0**n) for n in range(7)]
+
+
+COSINE = cosine_coefficients()
+
+
+def horner(coefficients, q):
+    value = q * coefficients[-1] + coefficients[-2]
+    for c in coefficients[-3::-1]:
+        value = value * q + c
+    return value
+
+
+def cosine_and_sine(r):
+    q = r * r
+    return horner(COSINE, q), horner(SINE, q) * r
 
 
 def sine_of_turns(turns):
@@ -71,6 +94,8 @@
     images_hbm,
     defocus_hbm,
     freq_hbm,
+    model_hbm,
+    index_hbm,
     kept_ref,
     other_ref,
     fine_sin,
@@ -78,6 +103,8 @@
     coarse_sin,
     coarse_cos,
     freq,
+    model,
+    index,
     pose,
     pose_row,
     images,
@@ -87,14 +114,15 @@
     step_sem,
     small_sems,
     image_sems,
-    counts,
-    *acc,
+    late_sems,
 ):
     count = images.shape[0]
     blocks = freq.shape[0]
     small = [
         pltpu.make_async_copy(src, dst, small_sems.at[n])
-        for n, (src, dst) in enumerate(((defocus_hbm, defocus), (freq_hbm, freq), (pose_hbm.at[0], pose), (pose_hbm, pose_row)))
+        for n, (src, dst) in enumerate(
+            ((defocus_hbm, defocus), (freq_hbm, freq), (pose_hbm.at[0], pose), (pose_hbm, pose_row))
+        )
     ]
     for copy in small:
         copy.start()
@@ -106,8 +134,7 @@
     lead = min(LEAD, count // piece)
     for j in range(lead):
         image_copy(j).start()
-    for part in acc:
-        part[...] = jnp.zeros_like(part)
+    kept_ref[...] = jnp.zeros_like(kept_ref)
     rows = lax.broadcasted_iota(jnp.int32, (2 * blocks, 2 * blocks), 0)
     cols = lax.broadcasted_iota(jnp.int32, (2 * blocks, 2 * blocks), 1)
     apart = jnp.where(cols == 2 * (rows % blocks) + rows // blocks, 1.0, 0.0).astype(bf16)
@@ -115,6 +142,12 @@
         copy.wait()
     for j in range(lead, count // piece):
         image_copy(j).start()
+    late = [
+        pltpu.make_async_copy(src, dst, late_sems.at[n])
+        for n, (src, dst) in enumerate(((model_hbm, model), (index_hbm, index)))
+    ]
+    for copy in late:
+        copy.start()
     side = lax.axis_index("slab") & 1
     step_row[...] = (defocus[...].astype(f32) * 8.0).astype(jnp.int32)
     step_copy = pltpu.make_async_copy(step_row.at[0], steps, step_sem)
@@ -133,7 +166,8 @@
     chosen = jnp.where(chosen, 1.0, 0.0).astype(bf16)
     named = (eighths & (LANES - 1)) == lax.broadcasted_iota(jnp.int32, (count, LANES), 1)
     named = jnp.where(named, 1.0, 0.0).astype(bf16)
-    counts[...] = jnp.dot(chosen, named, preferred_element_type=f32)
+    numbers = jnp.dot(chosen, named, preferred_element_type=f32)
+    kept_ref[:, 2 * blocks :] = numbers.reshape(bins, COUNT_ROWS, LANES)
     step_copy.wait()
 
     def one(image):
@@ -150,34 +184,38 @@
         for k in range(unroll):
             slot, s, both = one(unroll * j + k)
             for part, value in enumerate((s * both[:blocks], s * both[blocks:])):
-                acc[part][slot] += value
+                kept_ref[slot, part * blocks : (part + 1) * blocks] += value
         return 0
 
     lax.fori_loop(0, count // unroll, body, 0)
-    numbers = counts[...].reshape(bins, COUNT_ROWS, LANES)
-    for first, part in ((0, acc[0][...]), (blocks, acc[1][...]), (2 * blocks, numbers)):
-        rows = slice(first, first + part.shape[1])
-        kept_ref[:, rows] = part[:half]
-        other_ref[:, rows] = part[half:].astype(other_ref.dtype)
-
-
-def weighted_sums(images, defocus, pose_bin, freq_sq, bins):
+    other_ref[...] = kept_ref[half:].astype(other_ref.dtype)
+    for copy in late:
+        copy.wait()
+
+
+def weighted_sums(images, defocus, pose_bin, freq_sq, model_slice, block_index, bins):
     count, _, width = images.shape
     blocks = width // LANES
     half = bins // 2
     unroll, piece = 32, 16
     rows = images.reshape(count, 2, blocks, LANES).transpose(0, 2, 1, 3).reshape(count, 2 * blocks, LANES)
     height = 2 * blocks + COUNT_ROWS
+    model = model_slice.reshape(2, blocks, LANES).transpose(1, 0, 2).reshape(2 * blocks, LANES)
+    index = block_index[0].T
     return pl.pallas_call(
         functools.partial(sums_kernel, half, unroll, piece),
-        in_specs=[HBM] * 4,
-        out_specs=[VMEM] * 7,
+        in_specs=[HBM] * 6,
+        out_specs=[VMEM] * 9,
         out_shape=[
-            jax.ShapeDtypeStruct((half, height, LANES), f32),
+            jax.ShapeDtypeStruct((bins, height, LANES), f32),
             jax.ShapeDtypeStruct((half, height, LANES), bf16),
         ]
-        + [jax.ShapeDtypeStruct((n, blocks, LANES), f32) for n in (FINE, FINE, COARSE, COARSE)]
-        + [jax.ShapeDtypeStruct((blocks, LANES), f32)],
+        + [jax.ShapeDtypeStruct((n, blocks, LANES), f32) for n in (FINE, FINE, COARSE_USED, COARSE_USED)]
+        + [
+            jax.ShapeDtypeStruct((blocks, LANES), f32),
+            jax.ShapeDtypeStruct(model.shape, f32),
+            jax.ShapeDtypeStruct(index.shape, jnp.int32),
+        ],
         scratch_shapes=[
             pltpu.SMEM((count,), jnp.int32),
             pltpu.VMEM((1, count), jnp.int32),
@@ -188,30 +226,29 @@
             pltpu.SemaphoreType.DMA,
             pltpu.SemaphoreType.DMA((4,)),
             pltpu.SemaphoreType.DMA((count // piece,)),
-            pltpu.VMEM((bins * COUNT_ROWS, LANES), f32),
-            pltpu.VMEM((bins, blocks, LANES), f32),
-            pltpu.VMEM((bins, blocks, LANES), f32),
+            pltpu.SemaphoreType.DMA((2,)),
         ],
-        cost_estimate=pl.CostEstimate(flops=20 * 10**9, bytes_accessed=16 * 10**6, transcendentals=0),
         compiler_params=pltpu.CompilerParams(vmem_limit_bytes=24 * 2**20),
-    )(*in_hbm([pose_bin.reshape(1, -1), rows, defocus.reshape(1, -1), freq_sq.reshape(blocks, LANES)]))
+    )(
+        *in_hbm(
+            [
+                pose_bin.reshape(1, -1),
+                rows,
+                defocus.reshape(1, -1),
+                freq_sq.reshape(blocks, LANES),
+                model,
+                index,
+            ]
+        )
+    )
 
 
 def turn_by(cosine, sine, by):
     return cosine * by[0] - sine * by[1], sine * by[0] + cosine * by[1]
 
 
-def tables_kernel(
-    model_hbm, index_hbm, fine_sin, fine_cos, coarse_sin, coarse_cos, freq, model, index, fine, coarse, sems
-):
-    blocks = index.shape[1]
-    copies = [
-        pltpu.make_async_copy(src, dst, sems.at[n])
-        for n, (src, dst) in enumerate(((model_hbm, model), (index_hbm, index)))
-    ]
-    for copy in copies:
-        copy.start()
-
+def tables_kernel(fine_sin, fine_cos, coarse_sin, coarse_cos, freq, fine, coarse):
+    blocks = freq.shape[0]
     first = lax.broadcasted_iota(jnp.int32, (8, LANES), 0).astype(f32)
 
     def entry(cosines, sines, k, n):
@@ -222,7 +259,7 @@
         lanes = [pl.ds(pl.multiple_of((2 * k + part) * LANES, LANES), LANES) for part in range(2)]
         f = freq[pl.ds(k, 1), :]
         angle = first * (f * (0.125 / math.pi))
-        pair = [(sine_of_turns(angle + 0.25), sine_of_turns(angle))]
+        pair = [cosine_and_sine(angle)]
         by = entry(fine_cos, fine_sin, k, 16)
         for _ in range(FINE // 8 - 1):
             pair.append(turn_by(*pair[-1], by))
@@ -230,7 +267,7 @@
             fine[:, lanes[part]] = jnp.concatenate([p[part] for p in pair], axis=0).astype(bf16)
         angle = first * (f * (16.0 / math.pi))
         angle = angle - ((angle + ROUND) - ROUND)
-        even = (sine_of_turns(angle + 0.25), sine_of_turns(angle))
+        even = cosine_and_sine(angle)
         by = entry(coarse_cos, coarse_sin, k, 16)
         pair = [even, turn_by(*even, turn_by(*by, by))]
         by = entry(coarse_cos, coarse_sin, k, 2)
@@ -244,31 +281,19 @@
         return 0
 
     lax.fori_loop(0, blocks // GROUP, body, 0)
-    for copy in copies:
-        copy.wait()
-
-
-def tables(angles, model_slice, block_index):
-    blocks = block_index.shape[1]
-    model = model_slice.reshape(2, blocks, LANES).transpose(1, 0, 2).reshape(2 * blocks, LANES)
-    index = block_index[0].T
-    shapes = [
-        (model.shape, f32),
-        (index.shape, jnp.int32),
-        ((FINE, 2 * blocks * LANES), bf16),
-        ((COARSE, 2 * blocks * LANES), f32),
-    ]
+
+
+def tables(angles):
+    blocks = angles[-1].shape[0]
+    shapes = [((FINE, 2 * blocks * LANES), bf16), ((COARSE, 2 * blocks * LANES), f32)]
     return pl.pallas_call(
         tables_kernel,
-        in_specs=[HBM] * 2 + [VMEM] * 5,
-        out_specs=[VMEM] * 4,
+        in_specs=[VMEM] * 5,
+        out_specs=[VMEM] * 2,
         out_shape=[jax.ShapeDtypeStruct(shape, dtype) for shape, dtype in shapes],
-        scratch_shapes=[
-            pltpu.SemaphoreType.DMA((2,)),
-        ],
-        cost_estimate=pl.CostEstimate(flops=10**9, bytes_accessed=10**6, transcendentals=0),
+        cost_estimate=pl.CostEstimate(flops=20 * 10**9, bytes_accessed=16 * 10**6, transcendentals=0),
         compiler_params=pltpu.CompilerParams(vmem_limit_bytes=8 * 2**20),
-    )(*in_hbm([model, index]), *[a.reshape(-1, LANES) for a in angles])
+    )(*[a.reshape(-1, LANES) for a in angles])
 
 
 def volume_kernel(
@@ -321,7 +346,7 @@
     for j in range(touched):
         onehot = jnp.where(rows == index_ref[pl.ds(j, 1), :], 1.0, 0.0).astype(bf16)
         whole = terms[j]
-        for _ in range(3):
+        for _ in range(2):
             piece = whole.astype(bf16)
             whole = whole - piece.astype(f32)
             total = total + jnp.dot(onehot, piece, preferred_element_type=f32)
@@ -347,10 +372,13 @@
 def shards(images, defocus, pose_bin, freq_sq, model_slice, interp_coef, block_index, volume):
     slabs = lax.axis_size("slab")
     shells = lax.axis_size("shell")
-    kept, other, *angles = weighted_sums(images, defocus, pose_bin, freq_sq, slabs)
-    loaded = tables(angles, model_slice, block_index)
+    kept, other, *angles, model, index = weighted_sums(
+        images, defocus, pose_bin, freq_sq, model_slice, block_index, slabs
+    )
+    loaded = [model, index, *tables(angles)]
     other = lax.ppermute(other, "slab", [(i, i ^ 1) for i in range(slabs)])
-    pair = (kept + other.astype(f32)).astype(bf16)
+    half = slabs // 2
+    pair = (kept[:half] + other.astype(f32)).astype(bf16)
     pair, loaded = lax.optimization_barrier((pair, loaded))
     sums = lax.all_to_all(
         pair,

time: 39.2 us -> 38.9 us (level)
  Pallas kernels: 8.65 us -> 8.2 us
where the time goes in v3:
time: 38.9 us; the launch traced here: 38.8 us
  blocking collectives  29.2 us (75%)
  Pallas kernels  8.2 us (21%)
  local copies, waits for them, and re-layouts  0.66 us (2%)
  starting transfers between devices  0.52 us (1%)
    all_to_all x1, blocking collectives, shards(): lax.all_to_all(pair, 'slab', split_axis=0, concat_axis=0, tiled=True, axi...  17.9 us
    all_to_all x1, blocking collectives, shards(): lax.all_to_all(share, ('slab', 'shell'), split_axis=0, concat_axis=0, til...  11.4 us
    pallas_call x1, Pallas kernels, weighted_sums(): pl.pallas_call(functools.partial(sums_kernel, half, unroll, piece), in_sp...  4.58 us
    pallas_call x1, Pallas kernels, volume_share(): pl.pallas_call(functools.partial(volume_kernel, scale), in_specs=[VMEM] *...  2.06 us
    pallas_call x1, Pallas kernels, tables(): pl.pallas_call(tables_kernel, in_specs=[VMEM] * 5, out_specs=[VMEM] * 2,...  1.56 us
  transfers between devices with their start and end apart: 1, of which 0 were waited for; matrix products, arithmetic and copies ran while one was open for 0% of the time, Pallas kernels for 4%

profile of v3, /device:TPU:0, one launch (start us, length us, event | category | flops | bytes accessed | tf_op | source)
XLA Modules:
  0.0 38.8 jit_solution(6703014035364134241)
XLA Ops:
  0.0 4.6 %shard_map.73 = (f32[16,144,128]{2,1,0:T(8,128)S(1)}, bf16[8,144,128]{2,1,0:T(8,128)(2,1)S(1)}, f32[64,64,128]{2,1,0:T(8,128)S(1)}, f32[64,64,128]{2,1,0:T(8,128...) custom-call(s32[1,128]{1,0:T(1,128)} %bitcast.32, ...), custom_call_target="tpu_custom_call" | custom-call | tf_op jit(solution)/shard_map/pallas_call | solution.py:205
  4.6 0.5 %collective-permute-start = (bf16[8,144,128]{2,1,0:T(8,128)(2,1)S(1)}, bf16[8,144,128]{2,1,0:T(8,128)(2,1)S(1)}, u32[]{:S(2)}, u32[]{:S(2)}) collective-permute-start(bf16[8,144,128]{2,1,0:T(8,128)(2,1)S(1)} %get-tuple-element.22), channel_id=1, source_target_pairs={{0,2},{2,0},{4,6},{6,4},{8,10},{10,8},{12,14},{14,12},{16,18},{18,... | collective-permute-start | bytes 884744 | tf_op jit(solution)/shard_map/ppermute | solution.py:379
  5.1 0.0 slice-start
  5.1 0.0 slice-start.1
  5.1 1.6 %shard_map.74 = (bf16[64,16384]{1,0:T(8,128)(2,1)S(1)}, f32[32,16384]{1,0:T(8,128)S(1)}) custom-call(f32[4096,128]{1,0:T(8,128)S(1)} %bitcast.24, f32[4096,128]{1,0:T(8,128)S(1)} %bitcast.25, f32[1664,128]{1,0:T(8,128)S(1)} %bitcast.26, f32[1664,128]{1,0:T(8,128)S(1)} %bitcast.27, f32[64,128]{1,0:T(8,128)S(1)} %get-tuple-element.29.freq), custom_call_target="tpu_custom_call" | custom-call | flops 20000000000 | bytes 16000000 | tf_op jit(solution)/shard_map/pallas_call | solution.py:289
  6.7 0.0 collective-permute-done
  6.7 0.1 add_convert_fusion
  6.8 17.9 %all_to_all.14.sums_ref = bf16[8,144,128]{2,1,0:T(8,128)(2,1)S(1)} all-to-all(bf16[8,144,128]{2,1,0:T(8,128)(2,1)S(1)} %add_convert_fusion), channel_id=1, replica_groups={{0,4,8,12,16,20,24,28},{2,6,10,14,18,22,26,30},{1,5,9,13,17,21,25,29},{..., dimensions={0} | all-to-all | bytes 589824 | tf_op jit(solution)/shard_map/all_to_all | solution.py:383
  24.6 0.0 slice-done
  24.6 0.0 slice-done.1
  24.6 2.1 %shard_map.75 = f32[128,256]{1,0:T(8,128)S(1)} custom-call(bf16[8,144,128]{2,1,0:T(8,128)(2,1)S(1)} %all_to_all.14.sums_ref, f32[128,128]{1,0:T(8,128)S(1)} %get-tuple-element.33.model_ref, s32[4,64]{1,0:T(4,128)S(1)} %get-tuple-element.34.index_ref, bf16[64,16384]{1,0:T(8,128)(2,1)S(1)} %get-tuple-element.35.fine, ...), custom_call_target="tpu_custom_call" | custom-call | tf_op jit(solution)/shard_map/pallas_call | solution.py:358
  26.7 11.4 %all_to_all.15 = f32[32,4,256]{2,1,0:T(4,128)S(1)} all-to-all(f32[32,4,256]{2,1,0:T(4,128)S(1)} %all_to_all.10), channel_id=1, replica_groups=mesh['slab'=16,'shell'=2] {'slab','shell'}, dimensions={0} | all-to-all | bytes 262144 | tf_op jit(solution)/shard_map/all_to_all | solution.py:393
  38.2 0.6 %reduce_sum.12 = f32[4,2,128]{2,1,0:T(2,128)} reshape(f32[4,256]{1,0:T(4,128)S(1)} %reduce_sum.11) | data formatting | bytes 8192 | tf_op jit(solution)/shard_map/reduce_sum | solution.py:394
  (3 shorter events, 0.1 us)
Async XLA Ops:
  4.6 2.1 %collective-permute-start = (bf16[8,144,128]{2,1,0:T(8,128)(2,1)S(1)}, bf16[8,144,128]{2,1,0:T(8,128)(2,1)S(1)}, u32[]{:S(2)}, u32[]{:S(2)}) collective-permute-start(bf16[8,144,128]{2,1,0:T(8,128)(2,1)S(1)} %get-tuple-element.22), channel_id=1, source_target_pairs={{0,2},{2,0},{4,6},{6,4},{8,10},{10,8},{12,14},{14,12},{16,18},{18,... | collective-permute-start | bytes 884744 | tf_op jit(solution)/shard_map/ppermute | solution.py:379
  5.1 19.5 %slice-start = ((s8[8388608]{0:T(1024)(128)(4,1)}), s8[4194304]{0:T(1024)(128)(4,1)S(1)}, s32[]{:S(2)}) async-start(s8[8388608]{0:T(1024)(128)(4,1)} %bitcast.21), calls=%async_computation.2 | async-start | bytes 8388608
  5.1 19.5 %slice-start.1 = ((s8[8388608]{0:T(1024)(128)(4,1)}), s8[4194304]{0:T(1024)(128)(4,1)S(1)}, s32[]{:S(2)}) async-start(s8[8388608]{0:T(1024)(128)(4,1)} %bitcast.21), calls=%async_computation.3 | async-start | bytes 8388608

commit v4 on v3

--- a/solution.py
+++ b/solution.py
@@ -154,19 +154,14 @@
     step_copy.start()
     fill_table(fine_sin, fine_cos, freq[...] * (0.0625 / math.pi))
     fill_table(coarse_sin, coarse_cos, freq[...] * (4.0 / math.pi))
-    rows = lax.broadcasted_iota(jnp.int32, (count, count), 0)
-    cols = lax.broadcasted_iota(jnp.int32, (count, count), 1)
-    diagonal = jnp.where(rows == cols, defocus[...].astype(f32), 0.0).astype(bf16)
-    spread = jnp.dot(diagonal, jnp.ones((count, LANES), bf16), preferred_element_type=f32)
-    eighths = (spread * 8.0).astype(jnp.int32)
     bins = 2 * half
     place = ((pose_row[...] & 1) ^ side) * half + (pose_row[...] >> 1)
     place = place * COUNT_ROWS + (step_row[...] >> 7)
     chosen = lax.broadcasted_iota(jnp.int32, (bins * COUNT_ROWS, count), 0) == place
     chosen = jnp.where(chosen, 1.0, 0.0).astype(bf16)
-    named = (eighths & (LANES - 1)) == lax.broadcasted_iota(jnp.int32, (count, LANES), 1)
+    named = lax.broadcasted_iota(jnp.int32, (LANES, count), 0) == (step_row[...] & (LANES - 1))
     named = jnp.where(named, 1.0, 0.0).astype(bf16)
-    numbers = jnp.dot(chosen, named, preferred_element_type=f32)
+    numbers = lax.dot_general(chosen, named, (((1,), (1,)), ((), ())), preferred_element_type=f32)
     kept_ref[:, 2 * blocks :] = numbers.reshape(bins, COUNT_ROWS, LANES)
     step_copy.wait()
 
@@ -273,7 +268,7 @@
         by = entry(coarse_cos, coarse_sin, k, 2)
         pair += [turn_by(*p, by) for p in pair]
         coarse[:, lanes[0]] = jnp.concatenate([p[0] for p in pair], axis=0)
-        coarse[:, lanes[1]] = jnp.concatenate([-p[1] for p in pair], axis=0)
+        coarse[:, lanes[1]] = jnp.concatenate([p[1] for p in pair], axis=0)
 
     def body(j, _):
         for k in range(GROUP):
@@ -314,7 +309,7 @@
         cosine = (inner[:COARSE] + inner[COARSE:]) * coarse[:, lanes]
         cosine = sum(cosine[n : n + 8] for n in range(0, COARSE, 8))
         for k in range(GROUP):
-            both = cosine[:, 2 * k * LANES : (2 * k + 1) * LANES] + cosine[:, (2 * k + 1) * LANES : (2 * k + 2) * LANES]
+            both = cosine[:, 2 * k * LANES : (2 * k + 1) * LANES] - cosine[:, (2 * k + 1) * LANES : (2 * k + 2) * LANES]
             both = jnp.sum(both, axis=0, keepdims=True)
             power[first + k : first + k + 1, :] = (named - both) * 0.5
 

time: 38.9 us -> 38.7 us (level)
  no operation moved by 1% of the time
where the time goes in v4:
time: 38.7 us; the launch traced here: 38.6 us
  blocking collectives  29.2 us (75%)
  Pallas kernels  8.01 us (21%)
  local copies, waits for them, and re-layouts  0.66 us (2%)
  starting transfers between devices  0.53 us (1%)
    all_to_all x1, blocking collectives, shards(): lax.all_to_all(pair, 'slab', split_axis=0, concat_axis=0, tiled=True, axi...  17.9 us
    all_to_all x1, blocking collectives, shards(): lax.all_to_all(share, ('slab', 'shell'), split_axis=0, concat_axis=0, til...  11.3 us
    pallas_call x1, Pallas kernels, weighted_sums(): pl.pallas_call(functools.partial(sums_kernel, half, unroll, piece), in_sp...  4.46 us
    pallas_call x1, Pallas kernels, volume_share(): pl.pallas_call(functools.partial(volume_kernel, scale), in_specs=[VMEM] *...  2.06 us
    pallas_call x1, Pallas kernels, tables(): pl.pallas_call(tables_kernel, in_specs=[VMEM] * 5, out_specs=[VMEM] * 2,...  1.49 us
  transfers between devices with their start and end apart: 1, of which 0 were waited for; matrix products, arithmetic and copies ran while one was open for 0% of the time, Pallas kernels for 4%

profile of v4, /device:TPU:0, one launch (start us, length us, event | category | flops | bytes accessed | tf_op | source)
XLA Modules:
  0.0 38.6 jit_solution(16565198780592924589)
XLA Ops:
  0.0 4.5 %shard_map.73 = (f32[16,144,128]{2,1,0:T(8,128)S(1)}, bf16[8,144,128]{2,1,0:T(8,128)(2,1)S(1)}, f32[64,64,128]{2,1,0:T(8,128)S(1)}, f32[64,64,128]{2,1,0:T(8,128...) custom-call(s32[1,128]{1,0:T(1,128)} %bitcast.32, ...), custom_call_target="tpu_custom_call" | custom-call | tf_op jit(solution)/shard_map/pallas_call | solution.py:200
  4.5 0.5 %collective-permute-start = (bf16[8,144,128]{2,1,0:T(8,128)(2,1)S(1)}, bf16[8,144,128]{2,1,0:T(8,128)(2,1)S(1)}, u32[]{:S(2)}, u32[]{:S(2)}) collective-permute-start(bf16[8,144,128]{2,1,0:T(8,128)(2,1)S(1)} %get-tuple-element.22), channel_id=1, source_target_pairs={{0,2},{2,0},{4,6},{6,4},{8,10},{10,8},{12,14},{14,12},{16,18},{18,... | collective-permute-start | bytes 884744 | tf_op jit(solution)/shard_map/ppermute | solution.py:374
  5.0 0.0 slice-start
  5.0 0.0 slice-start.1
  5.0 1.5 %shard_map.74 = (bf16[64,16384]{1,0:T(8,128)(2,1)S(1)}, f32[32,16384]{1,0:T(8,128)S(1)}) custom-call(f32[4096,128]{1,0:T(8,128)S(1)} %bitcast.24, f32[4096,128]{1,0:T(8,128)S(1)} %bitcast.25, f32[1664,128]{1,0:T(8,128)S(1)} %bitcast.26, f32[1664,128]{1,0:T(8,128)S(1)} %bitcast.27, f32[64,128]{1,0:T(8,128)S(1)} %get-tuple-element.29.freq), custom_call_target="tpu_custom_call" | custom-call | flops 20000000000 | bytes 16000000 | tf_op jit(solution)/shard_map/pallas_call | solution.py:284
  6.5 0.0 collective-permute-done
  6.5 0.1 add_convert_fusion
  6.6 17.9 %all_to_all.14.sums_ref = bf16[8,144,128]{2,1,0:T(8,128)(2,1)S(1)} all-to-all(bf16[8,144,128]{2,1,0:T(8,128)(2,1)S(1)} %add_convert_fusion), channel_id=1, replica_groups={{0,4,8,12,16,20,24,28},{2,6,10,14,18,22,26,30},{1,5,9,13,17,21,25,29},{..., dimensions={0} | all-to-all | bytes 589824 | tf_op jit(solution)/shard_map/all_to_all | solution.py:378
  24.5 0.0 slice-done
  24.5 0.0 slice-done.1
  24.5 2.1 %shard_map.75 = f32[128,256]{1,0:T(8,128)S(1)} custom-call(bf16[8,144,128]{2,1,0:T(8,128)(2,1)S(1)} %all_to_all.14.sums_ref, f32[128,128]{1,0:T(8,128)S(1)} %get-tuple-element.33.model_ref, s32[4,64]{1,0:T(4,128)S(1)} %get-tuple-element.34.index_ref, bf16[64,16384]{1,0:T(8,128)(2,1)S(1)} %get-tuple-element.35.fine, ...), custom_call_target="tpu_custom_call" | custom-call | tf_op jit(solution)/shard_map/pallas_call | solution.py:353
  26.6 11.3 %all_to_all.15 = f32[32,4,256]{2,1,0:T(4,128)S(1)} all-to-all(f32[32,4,256]{2,1,0:T(4,128)S(1)} %all_to_all.10), channel_id=1, replica_groups=mesh['slab'=16,'shell'=2] {'slab','shell'}, dimensions={0} | all-to-all | bytes 262144 | tf_op jit(solution)/shard_map/all_to_all | solution.py:388
  38.0 0.6 %reduce_sum.12 = f32[4,2,128]{2,1,0:T(2,128)} reshape(f32[4,256]{1,0:T(4,128)S(1)} %reduce_sum.11) | data formatting | bytes 8192 | tf_op jit(solution)/shard_map/reduce_sum | solution.py:389
  (3 shorter events, 0.1 us)
Async XLA Ops:
  4.5 2.0 %collective-permute-start = (bf16[8,144,128]{2,1,0:T(8,128)(2,1)S(1)}, bf16[8,144,128]{2,1,0:T(8,128)(2,1)S(1)}, u32[]{:S(2)}, u32[]{:S(2)}) collective-permute-start(bf16[8,144,128]{2,1,0:T(8,128)(2,1)S(1)} %get-tuple-element.22), channel_id=1, source_target_pairs={{0,2},{2,0},{4,6},{6,4},{8,10},{10,8},{12,14},{14,12},{16,18},{18,... | collective-permute-start | bytes 884744 | tf_op jit(solution)/shard_map/ppermute | solution.py:374
  5.0 19.5 %slice-start = ((s8[8388608]{0:T(1024)(128)(4,1)}), s8[4194304]{0:T(1024)(128)(4,1)S(1)}, s32[]{:S(2)}) async-start(s8[8388608]{0:T(1024)(128)(4,1)} %bitcast.21), calls=%async_computation.2 | async-start | bytes 8388608
  5.0 19.5 %slice-start.1 = ((s8[8388608]{0:T(1024)(128)(4,1)}), s8[4194304]{0:T(1024)(128)(4,1)S(1)}, s32[]{:S(2)}) async-start(s8[8388608]{0:T(1024)(128)(4,1)} %bitcast.21), calls=%async_computation.3 | async-start | bytes 8388608

commit v5 on v4

--- a/solution.py
+++ b/solution.py
@@ -121,7 +121,7 @@
     small = [
         pltpu.make_async_copy(src, dst, small_sems.at[n])
         for n, (src, dst) in enumerate(
-            ((defocus_hbm, defocus), (freq_hbm, freq), (pose_hbm.at[0], pose), (pose_hbm, pose_row))
+            ((freq_hbm, freq), (defocus_hbm, defocus), (pose_hbm, pose_row), (pose_hbm.at[0], pose))
         )
     ]
     for copy in small:
@@ -138,7 +138,7 @@
     rows = lax.broadcasted_iota(jnp.int32, (2 * blocks, 2 * blocks), 0)
     cols = lax.broadcasted_iota(jnp.int32, (2 * blocks, 2 * blocks), 1)
     apart = jnp.where(cols == 2 * (rows % blocks) + rows // blocks, 1.0, 0.0).astype(bf16)
-    for copy in small:
+    for copy in small[:2]:
         copy.wait()
     for j in range(lead, count // piece):
         image_copy(j).start()
@@ -154,6 +154,8 @@
     step_copy.start()
     fill_table(fine_sin, fine_cos, freq[...] * (0.0625 / math.pi))
     fill_table(coarse_sin, coarse_cos, freq[...] * (4.0 / math.pi))
+    for copy in small[2:]:
+        copy.wait()
     bins = 2 * half
     place = ((pose_row[...] & 1) ^ side) * half + (pose_row[...] >> 1)
     place = place * COUNT_ROWS + (step_row[...] >> 7)

time: 38.7 us -> 38.4 us (level)
  no operation moved by 1% of the time
where the time goes in v5:
time: 38.4 us; the launch traced here: 38.2 us
  blocking collectives  29.2 us (76%)
  Pallas kernels  7.7 us (20%)
  local copies, waits for them, and re-layouts  0.66 us (2%)
  starting transfers between devices  0.51 us (1%)
    all_to_all x1, blocking collectives, shards(): lax.all_to_all(pair, 'slab', split_axis=0, concat_axis=0, tiled=True, axi...  17.9 us
    all_to_all x1, blocking collectives, shards(): lax.all_to_all(share, ('slab', 'shell'), split_axis=0, concat_axis=0, til...  11.3 us
    pallas_call x1, Pallas kernels, weighted_sums(): pl.pallas_call(functools.partial(sums_kernel, half, unroll, piece), in_sp...  4.15 us
    pallas_call x1, Pallas kernels, volume_share(): pl.pallas_call(functools.partial(volume_kernel, scale), in_specs=[VMEM] *...  2.06 us
    pallas_call x1, Pallas kernels, tables(): pl.pallas_call(tables_kernel, in_specs=[VMEM] * 5, out_specs=[VMEM] * 2,...  1.49 us
  transfers between devices with their start and end apart: 1, of which 0 were waited for; matrix products, arithmetic and copies ran while one was open for 0% of the time, Pallas kernels for 4%

profile of v5, /device:TPU:0, one launch (start us, length us, event | category | flops | bytes accessed | tf_op | source)
XLA Modules:
  0.0 38.2 jit_solution(10431064712860722688)
XLA Ops:
  0.0 4.2 %shard_map.73 = (f32[16,144,128]{2,1,0:T(8,128)S(1)}, bf16[8,144,128]{2,1,0:T(8,128)(2,1)S(1)}, f32[64,64,128]{2,1,0:T(8,128)S(1)}, f32[64,64,128]{2,1,0:T(8,128...) custom-call(s32[1,128]{1,0:T(1,128)} %bitcast.32, ...), custom_call_target="tpu_custom_call" | custom-call | tf_op jit(solution)/shard_map/pallas_call | solution.py:202
  4.2 0.5 %collective-permute-start = (bf16[8,144,128]{2,1,0:T(8,128)(2,1)S(1)}, bf16[8,144,128]{2,1,0:T(8,128)(2,1)S(1)}, u32[]{:S(2)}, u32[]{:S(2)}) collective-permute-start(bf16[8,144,128]{2,1,0:T(8,128)(2,1)S(1)} %get-tuple-element.22), channel_id=1, source_target_pairs={{0,2},{2,0},{4,6},{6,4},{8,10},{10,8},{12,14},{14,12},{16,18},{18,... | collective-permute-start | bytes 884744 | tf_op jit(solution)/shard_map/ppermute | solution.py:376
  4.7 0.0 slice-start
  4.7 0.0 slice-start.1
  4.7 1.5 %shard_map.74 = (bf16[64,16384]{1,0:T(8,128)(2,1)S(1)}, f32[32,16384]{1,0:T(8,128)S(1)}) custom-call(f32[4096,128]{1,0:T(8,128)S(1)} %bitcast.24, f32[4096,128]{1,0:T(8,128)S(1)} %bitcast.25, f32[1664,128]{1,0:T(8,128)S(1)} %bitcast.26, f32[1664,128]{1,0:T(8,128)S(1)} %bitcast.27, f32[64,128]{1,0:T(8,128)S(1)} %get-tuple-element.29.freq), custom_call_target="tpu_custom_call" | custom-call | flops 20000000000 | bytes 16000000 | tf_op jit(solution)/shard_map/pallas_call | solution.py:286
  6.2 0.0 collective-permute-done
  6.2 0.1 add_convert_fusion
  6.3 17.9 %all_to_all.14.sums_ref = bf16[8,144,128]{2,1,0:T(8,128)(2,1)S(1)} all-to-all(bf16[8,144,128]{2,1,0:T(8,128)(2,1)S(1)} %add_convert_fusion), channel_id=1, replica_groups={{0,4,8,12,16,20,24,28},{2,6,10,14,18,22,26,30},{1,5,9,13,17,21,25,29},{..., dimensions={0} | all-to-all | bytes 589824 | tf_op jit(solution)/shard_map/all_to_all | solution.py:380
  24.1 0.0 slice-done
  24.1 0.0 slice-done.1
  24.1 2.1 %shard_map.75 = f32[128,256]{1,0:T(8,128)S(1)} custom-call(bf16[8,144,128]{2,1,0:T(8,128)(2,1)S(1)} %all_to_all.14.sums_ref, f32[128,128]{1,0:T(8,128)S(1)} %get-tuple-element.33.model_ref, s32[4,64]{1,0:T(4,128)S(1)} %get-tuple-element.34.index_ref, bf16[64,16384]{1,0:T(8,128)(2,1)S(1)} %get-tuple-element.35.fine, ...), custom_call_target="tpu_custom_call" | custom-call | tf_op jit(solution)/shard_map/pallas_call | solution.py:355
  26.2 11.3 %all_to_all.15 = f32[32,4,256]{2,1,0:T(4,128)S(1)} all-to-all(f32[32,4,256]{2,1,0:T(4,128)S(1)} %all_to_all.10), channel_id=1, replica_groups=mesh['slab'=16,'shell'=2] {'slab','shell'}, dimensions={0} | all-to-all | bytes 262144 | tf_op jit(solution)/shard_map/all_to_all | solution.py:390
  37.6 0.6 %reduce_sum.12 = f32[4,2,128]{2,1,0:T(2,128)} reshape(f32[4,256]{1,0:T(4,128)S(1)} %reduce_sum.11) | data formatting | bytes 8192 | tf_op jit(solution)/shard_map/reduce_sum | solution.py:391
  (3 shorter events, 0.1 us)
Async XLA Ops:
  4.2 2.0 %collective-permute-start = (bf16[8,144,128]{2,1,0:T(8,128)(2,1)S(1)}, bf16[8,144,128]{2,1,0:T(8,128)(2,1)S(1)}, u32[]{:S(2)}, u32[]{:S(2)}) collective-permute-start(bf16[8,144,128]{2,1,0:T(8,128)(2,1)S(1)} %get-tuple-element.22), channel_id=1, source_target_pairs={{0,2},{2,0},{4,6},{6,4},{8,10},{10,8},{12,14},{14,12},{16,18},{18,... | collective-permute-start | bytes 884744 | tf_op jit(solution)/shard_map/ppermute | solution.py:376
  4.7 19.5 %slice-start = ((s8[8388608]{0:T(1024)(128)(4,1)}), s8[4194304]{0:T(1024)(128)(4,1)S(1)}, s32[]{:S(2)}) async-start(s8[8388608]{0:T(1024)(128)(4,1)} %bitcast.21), calls=%async_computation.2 | async-start | bytes 8388608
  4.7 19.5 %slice-start.1 = ((s8[8388608]{0:T(1024)(128)(4,1)}), s8[4194304]{0:T(1024)(128)(4,1)S(1)}, s32[]{:S(2)}) async-start(s8[8388608]{0:T(1024)(128)(4,1)} %bitcast.21), calls=%async_computation.3 | async-start | bytes 8388608
